TPU v7x, 32 devices: a whole 2x2x4 slice. The times are simulated.
32 devices in a mesh: space: 16 (over z, y, core), band: 2 (over x).
Axes of the slice: x: 2, y: 2, z: 4, core: 2. Of those that a mesh axis runs over, the one named last changes fastest.
Arguments:
- orbitals: float32 [320, 64, 512], P('band', 'space'), may hold values from -6 to 6
- potential: float32 [64, 512], P('space'), may hold values from -2 to 0
- rotation: float32 [320, 320], replicated, may hold values from -0.3125 to 0.3125
Outputs:
- rotated: float32 [320, 64, 512], P('band', 'space')
All inputs are finite; a program needn't handle non-finite values.
Results may differ from a plain program's by a relative error of at most 0.00007.
Values sent between devices are 32-bit elements; how exact they have to be, the bound alone decides.
A program may use at most 128 MiB of HBM per device.

v0:
```python
import jax
import jax.numpy as jnp
from jax import lax
from jax.sharding import PartitionSpec as P

DEG = 4
NY = 16
NZ = 32


coef_lap = (-205.0 / 72.0, 8.0 / 5.0, -1.0 / 5.0, 8.0 / 315.0, -1.0 / 560.0)
center_val = 6.0
half_width = 4.0


def with_halo(block, sides, width):
    for axis, dim in sides:
        count = lax.axis_size(axis)
        forward = [(i, i + 1) for i in range(count - 1)]
        forward.append((count - 1, 0))
        backward = [(target, source) for source, target in forward]
        low = lax.ppermute(
            lax.slice_in_dim(block, block.shape[dim] - width, None, axis=dim), axis, forward
        )
        high = lax.ppermute(lax.slice_in_dim(block, 0, width, axis=dim), axis, backward)
        block = jnp.concatenate([low, block, high], axis=dim)
    return block


def cross_terms(field):
    nblk, planes, cells = field.shape
    cube = field.reshape(nblk, planes, NY, NZ)
    inner = jnp.zeros_like(cube)
    for shift_k in range(1, 5):
        inner = inner + coef_lap[shift_k] * (
            jnp.roll(cube, shift_k, 2)
            + jnp.roll(cube, -shift_k, 2)
            + jnp.roll(cube, shift_k, 3)
            + jnp.roll(cube, -shift_k, 3)
        )
    return inner.reshape(nblk, planes, cells)


def hamil_slab(field, potential):
    planes = field.shape[1]
    padded = with_halo(field, (("space", 1),), 4)
    lap = 3.0 * coef_lap[0] * field
    for shift_k in range(1, 5):
        upper = padded[:, 4 + shift_k : 4 + shift_k + planes]
        lower = padded[:, 4 - shift_k : 4 - shift_k + planes]
        lap = lap + coef_lap[shift_k] * (upper + lower)
    lap = lap + cross_terms(field)
    return -0.5 * lap + potential[None] * field


def chebyshev(start_y, potential, apply_h):
    prev_y = start_y
    curr_y = (apply_h(start_y, potential) - center_val * start_y) / half_width
    for step in range(1, DEG):
        next_y = 2.0 * (apply_h(curr_y, potential) - center_val * curr_y) / half_width - prev_y
        prev_y = curr_y
        curr_y = next_y
    return curr_y


def local(orbitals, potential, rotation):
    curr_y = chebyshev(orbitals, potential, hamil_slab)
    turned = lax.dot_general(
        rotation,
        lax.all_to_all(curr_y, "band", split_axis=2, concat_axis=0, tiled=True),
        (((0,), (0,)), ((), ())),
        precision=lax.Precision.HIGHEST,
        preferred_element_type=jnp.float32,
    )
    return lax.all_to_all(turned, "band", split_axis=0, concat_axis=2, tiled=True)


def solution(mesh):
    placed = (P("band", "space", None), P("space", None), P())
    return jax.shard_map(
        local, mesh=mesh, in_specs=placed, out_specs=P("band", "space", None), check_vma=False
    )
```

profile of v0, /device:TPU:20, one launch (start us, length us, event | category | flops | bytes accessed | tf_op | source)
XLA Modules:
  0.0 293.6 jit_solution(2482150004143752801)
XLA Ops:
  0.0 2.9 copy.20
  3.4 1.8 copy.19
  8.1 1.5 fusion.190
  15.9 7.4 %fusion.83 = f32[160,4,16,32]{0,3,2,1:T(8,128)} fusion(f32[160,4,15,32]{0,3,2,1:T(8,128)S(1)} %get-tuple-element.132, f32[160,4,1,32]{0,3,2,1:T(8,128)} %get-tuple-element.134, f32[160,4,1,32]{0,3,2,1:T(8,128)} %get-tuple-element.133, f32[160,4,15,32]{0,3,2,1:T(8,128)S(1)} %get-tuple-element.131, f32[160,4,16,31]{0,3,2,1:T(8,128)S(1)} %get-tuple-element.128, ...), kind=kLoop, calls=%fused_computation.124 | loop fusion | flops 11468800 | bytes 22282240 | tf_op jit(solution)/shard_map/add | solution.py:35
  23.3 9.1 %collective-permute-done = f32[160,4,512]{2,0,1:T(8,128)} collective-permute-done((f32[160,4,512]{2,0,1:T(8,128)}, f32[160,4,512]{2,0,1:T(8,128)}, u32[]{:S(2)}, u32[]{:S(2)}) %collective-permute-start) | collective-permute-done | bytes 1310752 | tf_op jit(solution)/shard_map/ppermute | solution.py:25
  32.3 2.8 copy.22
  35.2 2.7 copy.24
  37.9 6.8 %broadcast_multiply_fusion = (f32[160,4,512]{0,2,1:T(8,128)S(1)}, f32[160,4,512]{0,2,1:T(8,128)}) fusion(f32[160,4,512]{0,2,1:T(8,128)S(1)} %copy.19, f32[4,512]{1,0:T(4,128)S(1)} %copy-done.20, f32[160,4,16,32]{0,3,2,1:T(8,128)} %fusion.83, f32[160,4,512]{0,2,1:T(8,128)} %copy.22, f32[160,4,512]{0,2,1:T(8,128)} %copy.24), kind=kLoop, calls=%fused_computation.195 | loop fusion | flops 8519680 | bytes 7872512 | tf_op jit(solution)/shard_map/div | solution.py:58
  44.8 2.6 fusion.172
  47.3 2.5 fusion.176
  49.8 2.4 fusion.180
  52.2 2.4 fusion.186
  54.6 2.3 fusion.182
  57.0 2.2 fusion.178
  59.2 2.0 fusion.174
  61.2 0.9 fusion.175
  63.8 0.9 fusion.177
  67.0 2.8 copy.31
  69.9 1.9 collective-permute-start.2
  75.4 10.0 %fusion.98 = f32[160,4,16,32]{0,3,2,1:T(8,128)} fusion(f32[160,4,15,32]{0,3,2,1:T(8,128)} %get-tuple-element.100, f32[160,4,1,32]{0,3,2,1:T(8,128)S(1)} %get-tuple-element.102, f32[160,4,1,32]{0,3,2,1:T(8,128)S(1)} %get-tuple-element.101, f32[160,4,15,32]{0,3,2,1:T(8,128)} %get-tuple-element.99, f32[160,4,16,31]{0,3,2,1:T(8,128)S(1)} %get-tuple-element.96, ...), kind=kLoop, calls=%fused_computation.143 | loop fusion | flops 11468800 | bytes 22282240 | tf_op jit(solution)/shard_map/add | solution.py:35
  85.4 13.6 %collective-permute-done.2 = f32[160,4,512]{2,0,1:T(8,128)} collective-permute-done((f32[160,4,512]{2,0,1:T(8,128)}, f32[160,4,512]{2,0,1:T(8,128)}, u32[]{:S(2)}, u32[]{:S(2)}) %collective-permute-start.2) | collective-permute-done | bytes 1310752 | tf_op jit(solution)/shard_map/ppermute | solution.py:25
  99.1 2.8 copy.32
  101.9 2.7 copy.34
  104.6 9.1 %fusion.47 = f32[160,4,512]{0,2,1:T(8,128)S(1)} fusion(f32[160,4,512]{0,2,1:T(8,128)} %copy-done.1, f32[160,4,512]{0,2,1:T(8,128)} %copy.34, f32[160,4,512]{0,2,1:T(8,128)} %copy-done.2, f32[160,4,512]{0,2,1:T(8,128)} %copy.32, f32[160,4,16,32]{0,3,2,1:T(8,128)} %fusion.98, f32[160,4,512]{0,2,1:T(8,128)} %get-tuple-element.6, ...), kind=kLoop, calls=%fused_computation.79 | loop fusion | flops 8847360 | bytes 9183232 | tf_op jit(solution)/shard_map/sub | solution.py:60
  113.7 2.5 fusion.156
  116.2 2.4 fusion.160
  118.6 2.4 fusion.164
  121.0 2.4 fusion.170
  123.4 2.3 fusion.166
  125.7 2.2 fusion.162
  127.9 2.1 fusion.158
  130.0 0.9 fusion.159
  132.6 0.9 fusion.161
  135.9 1.6 copy.38
  137.5 1.9 collective-permute-start.4
  143.0 10.0 %fusion.113 = f32[160,4,16,32]{0,3,2,1:T(8,128)} fusion(f32[160,4,15,32]{0,3,2,1:T(8,128)} %get-tuple-element.68, f32[160,4,1,32]{0,3,2,1:T(8,128)S(1)} %get-tuple-element.70, f32[160,4,1,32]{0,3,2,1:T(8,128)S(1)} %get-tuple-element.69, f32[160,4,15,32]{0,3,2,1:T(8,128)} %get-tuple-element.67, f32[160,4,16,31]{0,3,2,1:T(8,128)S(1)} %get-tuple-element.64, ...), kind=kLoop, calls=%fused_computation.162 | loop fusion | flops 11468800 | bytes 22282240 | tf_op jit(solution)/shard_map/add | solution.py:35
  153.0 13.6 %collective-permute-done.4 = f32[160,4,512]{2,0,1:T(8,128)} collective-permute-done((f32[160,4,512]{2,0,1:T(8,128)}, f32[160,4,512]{2,0,1:T(8,128)}, u32[]{:S(2)}, u32[]{:S(2)}) %collective-permute-start.4) | collective-permute-done | bytes 1310752 | tf_op jit(solution)/shard_map/ppermute | solution.py:25
  166.7 2.8 copy.39
  169.4 2.8 copy.41
  172.2 6.5 %fusion.29 = f32[160,4,512]{0,2,1:T(8,128)S(1)} fusion(f32[160,4,512]{0,2,1:T(8,128)} %copy.41, f32[160,4,512]{0,2,1:T(8,128)S(1)} %fusion.47, f32[160,4,512]{0,2,1:T(8,128)} %copy.39, f32[160,4,16,32]{0,3,2,1:T(8,128)} %fusion.113, f32[4,512]{1,0:T(4,128)S(1)} %copy-done.20, f32[160,4,512]{0,2,1:T(8,128)} %get-tuple-element.6), kind=kLoop, calls=%fused_computation.61 | loop fusion | flops 9175040 | bytes 7872512 | tf_op jit(solution)/shard_map/sub | solution.py:60
  178.8 2.7 fusion.144
  181.4 2.4 fusion.148
  183.9 2.4 fusion.152
  186.3 2.4 fusion.154
  188.6 2.3 fusion.150
  191.0 2.2 fusion.146
  193.1 2.1 fusion.142
  195.2 0.9 fusion.143
  197.7 0.9 fusion.145
  201.0 2.7 copy.44
  203.7 1.9 collective-permute-start.6
  205.6 1.0 fusion.155
  206.7 3.1 %fusion.140 = (f32[160,4,16,28]{0,3,2,1:T(8,128)S(1)}, f32[160,4,16,28]{0,3,2,1:T(8,128)S(1)}) fusion(f32[160,4,16,32]{0,3,2,1:T(8,128)} %bitcast.91), kind=kLoop, calls=%fused_computation.198 | loop fusion | bytes 4587520 | tf_op jit(solution)/shard_map/jit(_roll_static)/slice | solution.py:39
  211.4 10.0 %fusion.128 = f32[160,4,16,32]{0,3,2,1:T(8,128)} fusion(f32[160,4,15,32]{0,3,2,1:T(8,128)} %get-tuple-element.36, f32[160,4,1,32]{0,3,2,1:T(8,128)S(1)} %get-tuple-element.38, f32[160,4,1,32]{0,3,2,1:T(8,128)S(1)} %get-tuple-element.37, f32[160,4,15,32]{0,3,2,1:T(8,128)} %get-tuple-element.35, f32[160,4,16,31]{0,3,2,1:T(8,128)} %get-tuple-element.32, ...), kind=kLoop, calls=%fused_computation.181 | loop fusion | flops 11468800 | bytes 22282240 | tf_op jit(solution)/shard_map/add | solution.py:35
  221.4 13.7 %collective-permute-done.6 = f32[160,4,512]{2,0,1:T(8,128)} collective-permute-done((f32[160,4,512]{2,0,1:T(8,128)}, f32[160,4,512]{2,0,1:T(8,128)}, u32[]{:S(2)}, u32[]{:S(2)}) %collective-permute-start.6) | collective-permute-done | bytes 1310752 | tf_op jit(solution)/shard_map/ppermute | solution.py:25
  235.1 2.8 copy.45
  237.9 2.8 copy.47
  240.6 8.6 %fusion.11 = f32[160,4,512]{0,2,1:T(8,128)S(1)} fusion(f32[160,4,512]{0,2,1:T(8,128)S(1)} %fusion.47, f32[160,4,512]{0,2,1:T(8,128)} %copy.47, f32[160,4,512]{0,2,1:T(8,128)} %copy-done.4, f32[160,4,512]{0,2,1:T(8,128)} %copy.45, f32[160,4,16,32]{0,3,2,1:T(8,128)} %fusion.128, f32[4,512]{1,0:T(4,128)S(1)} %copy-done.20), kind=kLoop, calls=%fused_computation.43 | loop fusion | flops 8847360 | bytes 7872512 | tf_op jit(solution)/shard_map/sub | solution.py:60
  249.3 1.4 copy.50
  250.6 22.3 %all_to_all.36 = f32[160,4,512]{0,1,2:T(4,128)S(1)} all-to-all(f32[160,4,512]{0,1,2:T(4,128)S(1)} %copy.50), channel_id=1, replica_groups=mesh['space'=16,'band'=2] {'band'}, dimensions={2} | all-to-all | bytes 2621440 | tf_op jit(solution)/shard_map/all_to_all | solution.py:70
  273.0 1.6 copy.51
  274.6 3.6 %convolution_bitcast_fusion = f32[320,4,256]{2,0,1:T(8,128)S(1)} fusion(f32[320,4,256]{2,0,1:T(8,128)} %bitcast.93, f32[320,320]{1,0:T(8,128)S(1)} %copy-done), kind=kOutput, calls=%fused_computation.194 | convolution fusion | flops 1258291200 | bytes 3031040 | tf_op jit(solution)/shard_map/dot_general | solution.py:68
  279.1 13.3 %all_to_all.37 = f32[320,4,256]{2,1,0:T(4,128)S(1)} all-to-all(f32[320,4,256]{2,1,0:T(4,128)S(1)} %copy.53), channel_id=1, replica_groups=mesh['space'=16,'band'=2] {'band'}, dimensions={0} | all-to-all | bytes 2621440 | tf_op jit(solution)/shard_map/all_to_all | solution.py:75
  292.3 1.3 copy.57
  (87 shorter events, 31.5 us)
Async XLA Ops:
  0.0 274.6 %copy-start = (f32[320,320]{1,0:T(8,128)S(1)}, f32[320,320]{1,0:T(8,128)}, u32[]{:S(2)}) copy-start(f32[320,320]{1,0:T(8,128)} %param.5) | copy-start | bytes 1228804
  2.9 29.5 %collective-permute-start = (f32[160,4,512]{2,0,1:T(8,128)}, f32[160,4,512]{2,0,1:T(8,128)}, u32[]{:S(2)}, u32[]{:S(2)}) collective-permute-start(f32[160,4,512]{2,0,1:T(8,128)} %copy.20), channel_id=1, source_target_pairs={{2,0},{4,2},{6,4},{8,6},{10,8},{12,10},{14,12},{16,14},{18,16},{20... | collective-permute-start | bytes 3932168 | tf_op jit(solution)/shard_map/ppermute | solution.py:25
  2.9 32.3 %collective-permute-start.1 = (f32[160,4,512]{2,0,1:T(8,128)}, f32[160,4,512]{2,0,1:T(8,128)}, u32[]{:S(2)}, u32[]{:S(2)}) collective-permute-start(f32[160,4,512]{2,0,1:T(8,128)} %copy.20), channel_id=1, source_target_pairs={{0,2},{2,4},{4,6},{6,8},{8,10},{10,12},{12,14},{14,16},{16,18},{18... | collective-permute-start | bytes 3932168 | tf_op jit(solution)/shard_map/ppermute | solution.py:22
  5.2 32.8 %copy-start.1 = (f32[160,4,512]{0,2,1:T(8,128)}, f32[160,4,512]{0,2,1:T(8,128)S(1)}, u32[]{:S(2)}) copy-start(f32[160,4,512]{0,2,1:T(8,128)S(1)} %copy.19) | copy-start | bytes 3932164
  10.5 4.8 %copy-start.20 = (f32[4,512]{1,0:T(4,128)S(1)}, f32[4,512]{1,0:T(4,128)}, u32[]{:S(2)}) copy-start(f32[4,512]{1,0:T(4,128)} %param.4) | copy-start | bytes 24580
  44.8 21.5 %copy-start.2 = (f32[160,4,512]{0,2,1:T(8,128)}, f32[160,4,512]{0,2,1:T(8,128)S(1)}, u32[]{:S(2)}) copy-start(f32[160,4,512]{0,2,1:T(8,128)S(1)} %get-tuple-element.5) | copy-start | bytes 3932164
  67.0 4.8 %copy-start.3 = (f32[160,4,512]{0,2,1:T(8,128)S(1)}, f32[160,4,512]{0,2,1:T(8,128)}, u32[]{:S(2)}) copy-start(f32[160,4,512]{0,2,1:T(8,128)} %copy-done.2) | copy-start | bytes 3932164
  69.9 29.2 %collective-permute-start.2 = (f32[160,4,512]{2,0,1:T(8,128)}, f32[160,4,512]{2,0,1:T(8,128)}, u32[]{:S(2)}, u32[]{:S(2)}) collective-permute-start(f32[160,4,512]{2,0,1:T(8,128)} %copy.31), channel_id=1, source_target_pairs={{2,0},{4,2},{6,4},{8,6},{10,8},{12,10},{14,12},{16,14},{18,16},{20... | collective-permute-start | bytes 3932168 | tf_op jit(solution)/shard_map/ppermute | solution.py:25
  71.8 30.1 %collective-permute-start.3 = (f32[160,4,512]{2,0,1:T(8,128)}, f32[160,4,512]{2,0,1:T(8,128)}, u32[]{:S(2)}, u32[]{:S(2)}) collective-permute-start(f32[160,4,512]{2,0,1:T(8,128)} %copy.31), channel_id=1, source_target_pairs={{0,2},{2,4},{4,6},{6,8},{8,10},{10,12},{12,14},{14,16},{16,18},{18... | collective-permute-start | bytes 3932168 | tf_op jit(solution)/shard_map/ppermute | solution.py:22
  71.8 1.0 copy-start.17
  71.8 1.7 copy-start.5
  71.8 2.4 copy-start.6
  71.8 3.0 %copy-start.11 = (f32[160,4,16,29]{0,3,2,1:T(8,128)S(1)}, f32[160,4,16,29]{0,3,2,1:T(8,128)}, u32[]{:S(2)}) copy-start(f32[160,4,16,29]{0,3,2,1:T(8,128)} %get-tuple-element.79) | copy-start | bytes 3563524
  71.9 3.6 %copy-start.12 = (f32[160,4,16,29]{0,3,2,1:T(8,128)S(1)}, f32[160,4,16,29]{0,3,2,1:T(8,128)}, u32[]{:S(2)}) copy-start(f32[160,4,16,29]{0,3,2,1:T(8,128)} %get-tuple-element.80) | copy-start | bytes 3563524
  137.5 29.2 %collective-permute-start.4 = (f32[160,4,512]{2,0,1:T(8,128)}, f32[160,4,512]{2,0,1:T(8,128)}, u32[]{:S(2)}, u32[]{:S(2)}) collective-permute-start(f32[160,4,512]{2,0,1:T(8,128)} %copy.38), channel_id=1, source_target_pairs={{2,0},{4,2},{6,4},{8,6},{10,8},{12,10},{14,12},{16,14},{18,16},{20... | collective-permute-start | bytes 3932168 | tf_op jit(solution)/shard_map/ppermute | solution.py:25
  139.4 30.1 %collective-permute-start.5 = (f32[160,4,512]{2,0,1:T(8,128)}, f32[160,4,512]{2,0,1:T(8,128)}, u32[]{:S(2)}, u32[]{:S(2)}) collective-permute-start(f32[160,4,512]{2,0,1:T(8,128)} %copy.38), channel_id=1, source_target_pairs={{0,2},{2,4},{4,6},{6,8},{8,10},{10,12},{12,14},{14,16},{16,18},{18... | collective-permute-start | bytes 3932168 | tf_op jit(solution)/shard_map/ppermute | solution.py:22
  139.4 1.0 copy-start.18
  139.4 1.7 copy-start.7
  139.4 2.4 copy-start.8
  139.4 3.0 %copy-start.13 = (f32[160,4,16,29]{0,3,2,1:T(8,128)S(1)}, f32[160,4,16,29]{0,3,2,1:T(8,128)}, u32[]{:S(2)}) copy-start(f32[160,4,16,29]{0,3,2,1:T(8,128)} %get-tuple-element.47) | copy-start | bytes 3563524
  139.4 3.6 %copy-start.14 = (f32[160,4,16,29]{0,3,2,1:T(8,128)S(1)}, f32[160,4,16,29]{0,3,2,1:T(8,128)}, u32[]{:S(2)}) copy-start(f32[160,4,16,29]{0,3,2,1:T(8,128)} %get-tuple-element.48) | copy-start | bytes 3563524
  178.7 21.5 %copy-start.4 = (f32[160,4,512]{0,2,1:T(8,128)}, f32[160,4,512]{0,2,1:T(8,128)S(1)}, u32[]{:S(2)}) copy-start(f32[160,4,512]{0,2,1:T(8,128)S(1)} %fusion.29) | copy-start | bytes 3932164
  203.7 31.4 %collective-permute-start.6 = (f32[160,4,512]{2,0,1:T(8,128)}, f32[160,4,512]{2,0,1:T(8,128)}, u32[]{:S(2)}, u32[]{:S(2)}) collective-permute-start(f32[160,4,512]{2,0,1:T(8,128)} %copy.44), channel_id=1, source_target_pairs={{2,0},{4,2},{6,4},{8,6},{10,8},{12,10},{14,12},{16,14},{18,16},{20... | collective-permute-start | bytes 3932168 | tf_op jit(solution)/shard_map/ppermute | solution.py:25
  205.6 32.3 %collective-permute-start.7 = (f32[160,4,512]{2,0,1:T(8,128)}, f32[160,4,512]{2,0,1:T(8,128)}, u32[]{:S(2)}, u32[]{:S(2)}) collective-permute-start(f32[160,4,512]{2,0,1:T(8,128)} %copy.44), channel_id=1, source_target_pairs={{0,2},{2,4},{4,6},{6,8},{8,10},{10,12},{12,14},{14,16},{16,18},{18... | collective-permute-start | bytes 3932168 | tf_op jit(solution)/shard_map/ppermute | solution.py:22
  205.6 4.2 %copy-start.19 = (f32[160,4,4,32]{0,3,2,1:T(8,128)S(1)}, f32[160,4,4,32]{0,3,2,1:T(8,128)}, u32[]{:S(2)}) copy-start(f32[160,4,4,32]{0,3,2,1:T(8,128)} %get-tuple-element.14) | copy-start | bytes 983044
  206.7 3.1 %copy-start.9 = (f32[160,4,16,29]{0,3,2,1:T(8,128)S(1)}, f32[160,4,16,29]{0,3,2,1:T(8,128)}, u32[]{:S(2)}) copy-start(f32[160,4,16,29]{0,3,2,1:T(8,128)} %get-tuple-element.15) | copy-start | bytes 3563524
  206.7 3.5 %copy-start.10 = (f32[160,4,16,29]{0,3,2,1:T(8,128)S(1)}, f32[160,4,16,29]{0,3,2,1:T(8,128)}, u32[]{:S(2)}) copy-start(f32[160,4,16,29]{0,3,2,1:T(8,128)} %get-tuple-element.16) | copy-start | bytes 3563524
  206.7 4.1 %copy-start.15 = (f32[160,4,16,30]{0,3,2,1:T(8,128)S(1)}, f32[160,4,16,30]{0,3,2,1:T(8,128)}, u32[]{:S(2)}) copy-start(f32[160,4,16,30]{0,3,2,1:T(8,128)} %get-tuple-element.23) | copy-start | bytes 3686404
  206.7 4.7 %copy-start.16 = (f32[160,4,16,30]{0,3,2,1:T(8,128)S(1)}, f32[160,4,16,30]{0,3,2,1:T(8,128)}, u32[]{:S(2)}) copy-start(f32[160,4,16,30]{0,3,2,1:T(8,128)} %get-tuple-element.24) | copy-start | bytes 3686404
where the time goes:
time: 294 us
  local copies, waits for them, and re-layouts  129 us (44%)
  other arithmetic  68.4 us (23%)
  waiting for transfers between devices  50.1 us (17%)
  blocking collectives  35.6 us (12%)
  starting transfers between devices  6.24 us (2%)
  matrix products  3.62 us (1%)
    ppermute x4, waiting for transfers between devices, with_halo(): lax.ppermute(lax.slice_in_dim(block, 0, width, axis=dim), axis, backward)  50.1 us
    slice x32, local copies, waits for them, and re-layouts, cross_terms(): jnp.roll(cube, -shift_k, 3)  41.7 us
    slice x32, local copies, waits for them, and re-layouts, cross_terms(): jnp.roll(cube, -shift_k, 2)  40.8 us
    add x4, other arithmetic, cross_terms(): inner + coef_lap[shift_k] * (jnp.roll(cube, shift_k, 2) + jnp.roll(cube,...  37.3 us
    sub x3, other arithmetic, chebyshev(): 2.0 * (apply_h(curr_y, potential) - center_val * curr_y) / half_width  24.2 us
    all_to_all x1, blocking collectives, local(): lax.all_to_all(curr_y, 'band', split_axis=2, concat_axis=0, tiled=True)  22.3 us
    all_to_all x1, blocking collectives, local(): lax.all_to_all(turned, 'band', split_axis=0, concat_axis=2, tiled=True)  13.3 us
    unnamed x44, local copies, waits for them, and re-layouts  12.4 us
  transfers between devices with their start and end apart: 8, of which 4 were waited for; matrix products, arithmetic and copies ran while one was open for 23% of the time, Pallas kernels for 0%

commit v1 on v0

--- a/solution.py
+++ b/solution.py
@@ -1,16 +1,29 @@
+import functools
+
 import jax
 import jax.numpy as jnp
+import numpy as np
 from jax import lax
+from jax.experimental import pallas as pl
+from jax.experimental.pallas import tpu as pltpu
 from jax.sharding import PartitionSpec as P
 
 DEG = 4
 NY = 16
 NZ = 32
+MESH = pl.DeviceIdType.MESH
 
 
 coef_lap = (-205.0 / 72.0, 8.0 / 5.0, -1.0 / 5.0, 8.0 / 315.0, -1.0 / 560.0)
 center_val = 6.0
 half_width = 4.0
+
+MAIN = 8
+REST = 2
+SLAB = 4
+CELLS = NY * NZ
+WEIGHT = [-0.5 * c / half_width for c in coef_lap]
+SHIFT = -1.5 * coef_lap[0] - center_val
 
 
 def with_halo(block, sides, width):
@@ -63,7 +76,7 @@
     return curr_y
 
 
-def local(orbitals, potential, rotation):
+def local_halo(orbitals, potential, rotation):
     curr_y = chebyshev(orbitals, potential, hamil_slab)
     turned = lax.dot_general(
         rotation,
@@ -75,6 +88,372 @@
     return lax.all_to_all(turned, "band", split_axis=0, concat_axis=2, tiled=True)
 
 
+def split_const(matrix):
+    high = matrix.astype(np.float32).astype(jnp.bfloat16)
+    low = (matrix - high.astype(np.float64)).astype(np.float32).astype(jnp.bfloat16)
+    return np.stack([high, low])
+
+
+def ring_matrix(size):
+    ring = np.zeros((size, size))
+    for at in range(size):
+        for k in range(1, 5):
+            ring[at, (at + k) % size] += WEIGHT[k]
+            ring[at, (at - k) % size] += WEIGHT[k]
+    return ring
+
+
+def in_plane():
+    return split_const(
+        np.kron(ring_matrix(NY), np.eye(NZ)) + np.kron(np.eye(NY), ring_matrix(NZ))
+    )
+
+
+def across_planes(planes):
+    return split_const(np.kron(ring_matrix(planes), np.eye(REST)))
+
+
+def spread(planes):
+    rows = np.concatenate(
+        [np.repeat(np.arange(planes), MAIN), np.repeat(np.arange(planes), REST)]
+    )
+    picks = np.arange(2 * planes)
+    return np.stack([rows[:, None] * 2 + half == picks[None] for half in range(2)]).astype(
+        jnp.bfloat16
+    )
+
+
+def split2(value):
+    high = value.astype(jnp.bfloat16)
+    low = (value - high.astype(jnp.float32)).astype(jnp.bfloat16)
+    return high, low
+
+
+def dot(a, b):
+    return jnp.dot(a, b, preferred_element_type=jnp.float32)
+
+
+def kernel(
+    n,
+    y_ref,
+    rt_ref,
+    pot_ref,
+    plane_hbm,
+    cross_ref,
+    spread_ref,
+    out_ref,
+    other,
+    turned,
+    buf0,
+    buf1,
+    buf2,
+    rest_send,
+    rest_in,
+    rest_out,
+    rest_back,
+    pots,
+    diag,
+    plane,
+    acc,
+    high,
+    low,
+    x_send,
+    x_recv,
+    pot_send,
+    pot_recv,
+    a_send,
+    a_recv,
+    b_send,
+    b_recv,
+    oa_send,
+    oa_recv,
+    ob_send,
+    ob_recv,
+    plane_sem,
+):
+    me = lax.axis_index("space")
+    band = lax.axis_index("band")
+    nx = SLAB * n
+    rows = nx * MAIN
+    first_rest = MAIN * n
+
+    barrier = pltpu.get_barrier_semaphore()
+    pl.semaphore_signal(
+        barrier, inc=1, device_id={"band": 1 - band}, device_id_type=MESH
+    )
+
+    def peers(body):
+        def step(k, carry):
+            body(lax.rem(me + k, n))
+            return carry
+
+        lax.fori_loop(1, n, step, 0)
+
+    peers(
+        lambda d: pl.semaphore_signal(
+            barrier, inc=1, device_id={"space": d}, device_id_type=MESH
+        )
+    )
+    plane_copy = pltpu.make_async_copy(plane_hbm, plane, plane_sem)
+    plane_copy.start()
+    pl.semaphore_wait(barrier, n)
+
+    def x_copy(p):
+        return pltpu.make_async_remote_copy(
+            src_ref=y_ref.at[p],
+            dst_ref=other.at[p],
+            send_sem=x_send.at[p],
+            recv_sem=x_recv.at[p],
+            device_id={"band": 1 - band},
+            device_id_type=MESH,
+        )
+
+    def space_copy(src, dst, send_sem, recv_sem, target):
+        return pltpu.make_async_remote_copy(
+            src_ref=src,
+            dst_ref=dst,
+            send_sem=send_sem,
+            recv_sem=recv_sem,
+            device_id={"space": target},
+            device_id_type=MESH,
+        )
+
+    def main_rows(d):
+        return pl.ds(pl.multiple_of(MAIN * d, MAIN), MAIN)
+
+    def pot_copy(d, at):
+        return space_copy(pot_ref, pots.at[at], pot_send.at[d], pot_recv.at[at], d)
+
+    def a_plane(d, at, p):
+        return space_copy(
+            turned.at[p, main_rows(d), :],
+            buf0.at[4 + SLAB * at + p],
+            a_send.at[d],
+            a_recv.at[at],
+            d,
+        )
+
+    def a_whole(d, at):
+        return space_copy(
+            turned.at[:, main_rows(d), :],
+            buf0.at[pl.ds(4 + SLAB * at, SLAB)],
+            a_send.at[d],
+            a_recv.at[at],
+            d,
+        )
+
+    def b_copy(d, at):
+        return space_copy(rest_send.at[d], rest_in.at[at], b_send.at[d], b_recv.at[at], d)
+
+    def oa_copy(d, at):
+        return space_copy(
+            buf1.at[pl.ds(4 + SLAB * d, SLAB)],
+            out_ref.at[:, main_rows(at), :],
+            oa_send.at[d],
+            oa_recv.at[at],
+            d,
+        )
+
+    def ob_copy(d, at):
+        return space_copy(rest_out.at[d], rest_back.at[at], ob_send.at[d], ob_recv.at[at], d)
+
+    for p in range(SLAB):
+        x_copy(p).start()
+    peers(lambda d: pot_copy(d, me).start())
+    pots[me] = pot_ref[...]
+
+    own_high, own_low = split2(rt_ref[0])
+    oth_high, oth_low = split2(rt_ref[1])
+    for p in range(SLAB):
+        vh, vl = split2(y_ref[p])
+        turned[p] = dot(own_high, vh) + dot(own_high, vl) + dot(own_low, vh)
+    for p in range(SLAB):
+        x_copy(p).wait_recv()
+        vh, vl = split2(other[p])
+        turned[p] += dot(oth_high, vh) + dot(oth_high, vl) + dot(oth_low, vh)
+        peers(lambda d, p=p: a_plane(d, me, p).start())
+        buf0[4 + SLAB * me + p] = turned[p, main_rows(me), :]
+        for d in range(n):
+            rest_send[d, REST * p : REST * p + REST, :] = turned[
+                p, first_rest + REST * d : first_rest + REST * d + REST, :
+            ]
+    peers(lambda d: b_copy(d, me).start())
+    rest_in[me] = rest_send[me]
+
+    peers(lambda s: pot_copy(s, s).wait_recv())
+    field = pots[...].reshape(2 * nx, CELLS // 2)
+    fh, rem = field.astype(jnp.bfloat16), field
+    rem = rem - fh.astype(jnp.float32)
+    fm, fl = split2(rem)
+    for half in range(2):
+        pick = spread_ref[half]
+        diag[:, half * (CELLS // 2) : (half + 1) * (CELLS // 2)] = (
+            dot(pick, fh) + dot(pick, fm) + dot(pick, fl) + SHIFT
+        ) * (1.0 / half_width)
+
+    plane_copy.wait()
+
+    def wrap(ref):
+        ref[0:4] = ref[nx : nx + 4]
+        ref[nx + 4 : nx + 8] = ref[4:8]
+
+    def put_split(g, lanes, value):
+        flat = value.reshape(8 * MAIN, 128)
+        hi, lo = split2(flat)
+        at = pl.ds(pl.multiple_of(g * (8 * MAIN), 8 * MAIN), 8 * MAIN)
+        high[at, lanes] = hi
+        low[at, lanes] = lo
+
+    def each_group(body):
+        def step(g, carry):
+            for c in range(CELLS // 128):
+                body(g, slice(128 * c, 128 * c + 128))
+            return carry
+
+        lax.fori_loop(0, nx // 8, step, 0)
+
+    peers(lambda s: a_whole(s, s).wait_recv())
+    wrap(buf0)
+    each_group(
+        lambda g, lanes: put_split(g, lanes, buf0[pl.ds(g * 8 + 4, 8), :, lanes])
+    )
+    block = min(rows, 256)
+    order = [(buf0, None, buf1), (buf1, buf0, buf2), (buf2, buf1, buf0), (buf0, buf2, buf1)]
+    for number, (cur, prev, new) in enumerate(order):
+        last = number == DEG - 1
+        for r in range(rows // block):
+            at = slice(r * block, (r + 1) * block)
+            acc[at, :] = (
+                dot(high[at, :], plane[0]) + dot(low[at, :], plane[0]) + dot(high[at, :], plane[1])
+            )
+
+        def update(g, lanes, cur=cur, prev=prev, new=new, last=last):
+            wide = cur[pl.ds(g * 8, 16), :, lanes]
+            at = pl.ds(pl.multiple_of(g * (8 * MAIN), 8 * MAIN), 8 * MAIN)
+            total = acc[at, lanes].reshape(8, MAIN, 128)
+            total = total + diag[at, lanes].reshape(8, MAIN, 128) * wide[4:12]
+            for k in range(1, 5):
+                total = total + WEIGHT[k] * (wide[4 + k : 12 + k] + wide[4 - k : 12 - k])
+            if prev is not None:
+                total = 2.0 * total - prev[pl.ds(g * 8 + 4, 8), :, lanes]
+            new[pl.ds(g * 8 + 4, 8), :, lanes] = total
+            if not last:
+                put_split(g, lanes, total)
+
+        each_group(update)
+        if not last:
+            wrap(new)
+    peers(lambda d: oa_copy(d, me).start())
+    out_ref[:, main_rows(me), :] = buf1[pl.ds(4 + SLAB * me, SLAB)]
+
+    peers(lambda s: b_copy(s, s).wait_recv())
+    cur = rest_in[...].reshape(nx * REST, CELLS)
+    prev = None
+    weight = diag[rows : rows + nx * REST, :]
+    for number in range(DEG):
+        vh, vl = split2(cur)
+        total = (
+            dot(vh, plane[0])
+            + dot(vl, plane[0])
+            + dot(vh, plane[1])
+            + dot(cross_ref[0], vh)
+            + dot(cross_ref[0], vl)
+            + dot(cross_ref[1], vh)
+            + weight * cur
+        )
+        if prev is not None:
+            total = 2.0 * total - prev
+        prev, cur = cur, total
+    rest_out[...] = cur.reshape(n, SLAB * REST, CELLS)
+    peers(lambda d: ob_copy(d, me).start())
+    rest_back[me] = rest_out[me]
+
+    peers(lambda s: oa_copy(s, s).wait_recv())
+    peers(lambda s: ob_copy(s, s).wait_recv())
+    for p in range(SLAB):
+        for d in range(n):
+            out_ref[p, first_rest + REST * d : first_rest + REST * d + REST, :] = rest_back[
+                d, REST * p : REST * p + REST, :
+            ]
+    for p in range(SLAB):
+        x_copy(p).wait_send()
+
+    def drain(d):
+        pot_copy(d, me).wait_send()
+        a_whole(d, me).wait_send()
+        b_copy(d, me).wait_send()
+        oa_copy(d, me).wait_send()
+        ob_copy(d, me).wait_send()
+
+    peers(drain)
+
+
+def local_whole(orbitals, potential, rotation):
+    n = lax.axis_size("space")
+    band = lax.axis_index("band")
+    held = orbitals.shape[0]
+    nx = SLAB * n
+    rows = nx * MAIN
+    columns = lax.dynamic_slice_in_dim(rotation, band * held, held, axis=1)
+    own = lax.dynamic_slice_in_dim(columns, band * held, held, axis=0)
+    oth = lax.dynamic_slice_in_dim(columns, (1 - band) * held, held, axis=0)
+    turn = jnp.stack([own.T, oth.T])
+    f32, bf16 = jnp.float32, jnp.bfloat16
+    vmem = pl.BlockSpec(memory_space=pltpu.VMEM)
+    tile = (n, SLAB * REST, CELLS)
+    sems = pltpu.SemaphoreType.DMA((n,))
+    result = pl.pallas_call(
+        functools.partial(kernel, n),
+        out_shape=jax.ShapeDtypeStruct((SLAB, held, CELLS), f32),
+        in_specs=[vmem, vmem, vmem, pl.BlockSpec(memory_space=pl.ANY), vmem, vmem],
+        out_specs=vmem,
+        scratch_shapes=[
+            pltpu.VMEM((SLAB, held, CELLS), f32),
+            pltpu.VMEM((SLAB, held, CELLS), f32),
+            pltpu.VMEM((nx + 8, MAIN, CELLS), f32),
+            pltpu.VMEM((nx + 8, MAIN, CELLS), f32),
+            pltpu.VMEM((nx + 8, MAIN, CELLS), f32),
+            pltpu.VMEM(tile, f32),
+            pltpu.VMEM(tile, f32),
+            pltpu.VMEM(tile, f32),
+            pltpu.VMEM(tile, f32),
+            pltpu.VMEM((n, 2 * SLAB, CELLS // 2), f32),
+            pltpu.VMEM((nx * (MAIN + REST), CELLS), f32),
+            pltpu.VMEM((2, CELLS, CELLS), bf16),
+            pltpu.VMEM((rows, CELLS), f32),
+            pltpu.VMEM((rows, CELLS), bf16),
+            pltpu.VMEM((rows, CELLS), bf16),
+            pltpu.SemaphoreType.DMA((SLAB,)),
+            pltpu.SemaphoreType.DMA((SLAB,)),
+            sems, sems, sems, sems, sems, sems, sems, sems, sems, sems,
+            pltpu.SemaphoreType.DMA,
+        ],
+        compiler_params=pltpu.CompilerParams(
+            collective_id=0, has_side_effects=True, vmem_limit_bytes=40 * 1024 * 1024
+        ),
+    )(
+        jnp.transpose(orbitals, (1, 0, 2)),
+        turn,
+        potential.reshape(2 * SLAB, CELLS // 2),
+        jnp.asarray(in_plane()),
+        jnp.asarray(across_planes(nx)),
+        jnp.asarray(spread(nx)),
+    )
+    return jnp.transpose(result, (1, 0, 2))
+
+
+def local(orbitals, potential, rotation):
+    n = lax.axis_size("space")
+    fits = (
+        lax.axis_size("band") == 2
+        and n > 1
+        and orbitals.shape == ((MAIN + REST) * n, SLAB, CELLS)
+    )
+    if fits:
+        return local_whole(orbitals, potential, rotation)
+    return local_halo(orbitals, potential, rotation)
+
+
 def solution(mesh):
     placed = (P("band", "space", None), P("space", None), P())
     return jax.shard_map(

time: 294 us -> 88.4 us (0.30)
  the two profiles are of different devices: /device:TPU:20 before, /device:TPU:25 now
where the time goes in v1:
time: 88.4 us; the launch traced here: 88.2 us
  Pallas kernels  82.7 us (94%)
  local copies, waits for them, and re-layouts  5.4 us (6%)
    pallas_call x1, Pallas kernels, local_whole(): pl.pallas_call(functools.partial(kernel, n), out_shape=jax.ShapeDtypeStru...  82.7 us
    transpose x1, local copies, waits for them, and re-layouts, local_whole(): return jnp.transpose(result, (1, 0, 2))  1.9 us

profile of v1, /device:TPU:25, one launch (start us, length us, event | category | flops | bytes accessed | tf_op | source)
XLA Modules:
  0.0 88.2 jit_solution(6880394021075455807)
XLA Ops:
  0.0 0.0 copy-start.3
  0.0 0.8 reshape.3.pot_ref
  0.8 1.2 %fusion = (f32[160,160]{1,0:T(8,128)S(1)}, f32[160,160]{1,0:T(8,128)S(1)}) fusion(f32[320,320]{1,0:T(8,128)} %param.8, s32[]{:T(128)S(6)} %select_n.12, s32[]{:T(128)S(6)} %select_n.14), kind=kLoop, calls=%fused_computation.2 | loop fusion | bytes 409608 | tf_op jit(solution)/shard_map/dynamic_slice | solution.py:398
  2.0 0.1 copy.11
  2.1 0.1 copy.12
  2.3 0.0 copy-done.3
  2.3 0.0 copy-start
  2.3 0.0 copy-start.1
  2.3 0.0 copy-start.2
  2.3 0.4 copy.14
  2.8 0.8 copy-done
  3.5 0.1 copy-done.1
  3.6 0.0 copy-done.2
  3.6 82.7 %shard_map.64 = f32[4,160,512]{2,1,0:T(8,128)S(1)} custom-call(f32[4,160,512]{2,1,0:T(8,128)S(1)} %bitcast.11, f32[2,160,160]{2,1,0:T(8,128)S(1)} %pad_maximum_fusion.rt_ref, f32[8,256]{1,0:T(8,128)S(1)} %reshape.3.pot_ref, bf16[2,512,512]{2,1,0:T(8,128)(2,1)S(1)} %copy-done, bf16[2,128,128]{2,1,0:T(8,128)(2,1)S(1)} %copy-done.2, ...), custom_call_target="tpu_custom_call" | custom-call | tf_op jit(solution)/shard_map/pallas_call | solution.py:405
  86.3 1.9 %copy.10 = f32[160,4,512]{2,1,0:T(4,128)} copy(f32[160,4,512]{2,0,1:T(8,128)S(1)} %bitcast.10) | data formatting | bytes 2621440 | tf_op jit(solution)/shard_map/transpose | solution.py:442
  (1 shorter events, 0.0 us)
Async XLA Ops:
  0.0 2.3 %copy-start.3 = (f32[160,4,512]{2,1,0:T(4,128)S(1)}, f32[160,4,512]{2,1,0:T(4,128)}, u32[]{:S(2)}) copy-start(f32[160,4,512]{2,1,0:T(4,128)} %param.6) | copy-start | bytes 3932164
  2.3 1.2 %copy-start = (bf16[2,512,512]{2,1,0:T(8,128)(2,1)S(1)}, bf16[2,512,512]{2,1,0:T(8,128)(2,1)}, u32[]{:S(2)}) copy-start(bf16[2,512,512]{2,1,0:T(8,128)(2,1)} %constant.38.clone.plane_hbm) | copy-start | bytes 3145732
  2.3 1.3 %copy-start.1 = (bf16[2,640,128]{2,1,0:T(8,128)(2,1)S(1)}, bf16[2,640,128]{2,1,0:T(8,128)(2,1)}, u32[]{:S(2)}) copy-start(bf16[2,640,128]{2,1,0:T(8,128)(2,1)} %constant.40.clone.spread_ref) | copy-start | bytes 983044
  2.3 1.3 %copy-start.2 = (bf16[2,128,128]{2,1,0:T(8,128)(2,1)S(1)}, bf16[2,128,128]{2,1,0:T(8,128)(2,1)}, u32[]{:S(2)}) copy-start(bf16[2,128,128]{2,1,0:T(8,128)(2,1)} %constant.39.clone.cross_ref) | copy-start | bytes 196612
